TPU v7x, 32 devices: a whole 2x2x4 slice. The times are simulated.
32 devices in a mesh: group: 2 (over x), tile: 16 (over z, y, core).
Axes of the slice: x: 2, y: 2, z: 4, core: 2. Of those that a mesh axis runs over, the one named last changes fastest.
Arguments:
- gains: float32 [32768, 64], P(('group', 'tile')), parts along dimension 0, may hold values from -6 to 6
- tiles: int32 [256, 3], P(('group', 'tile')), parts along dimension 0, may hold values from 0 to 15, as said below
- vis: bfloat16 [256, 2, 32, 1024], P(('group', 'tile')), parts along dimension 0, may hold values from -24 to 24
- flags: int32 [256, 1024], P(('group', 'tile')), parts along dimension 0, may hold values 0 or 1
- station_uvw: float32 [32, 3, 512], P('group'), parts along dimension 0, may hold values from -1000 to 1000
- src_lm: float32 [2, 32], replicated, may hold values from -0.02 to 0.02
- flux: float32 [32, 32], replicated, may hold values from 0.2 to 2
Outputs:
- gains_out: float32 [32768, 64], P(('group', 'tile')), parts along dimension 0
There are 2 independent parts, one for each index of `group`. A program takes and returns all parts, laid end to end along the dimension named above; an argument that names none is the same for every part. Nothing has to cross between parts.
Inputs may be any that keep to these rules, and one draw needn't show every extreme that they name: `tiles`: each row is (row block, column block, time step) of one item; the row block is at least the column block, both below 16, and the time step is below 16.
All inputs are finite; a program needn't handle non-finite values. No bound on the sum of `flags` on one device may be relied on, other than what follows from the above.
Results may differ from a plain program's by a relative error of at most 0.0013.
Values sent between devices are 32-bit elements; how exact they have to be, the bound alone decides.
A program may use at most 192 MiB of HBM per device.

v0:
```python
import math

import jax
import jax.numpy as jnp
from jax import lax
from jax.sharding import PartitionSpec as P

STATIONS = 512
DIRS = 32
CHANS = 32
SB = 32
ITERS = 2


highest = lax.Precision.HIGHEST


def product(form, left, right):
    return jnp.einsum(form, left, right, precision=highest)


def rotate(positions, gain_block, source_l, source_m, source_n, frequency):
    delays = (
        positions[:, 0, :, None] * source_l
        + positions[:, 1, :, None] * source_m
        + positions[:, 2, :, None] * source_n
    )
    phases = 2.0 * math.pi * delays[:, None, :, :] * frequency[None, :, None, None]
    cosine = jnp.cos(phases)
    sine_part = jnp.sin(phases)
    gain_re = jnp.transpose(gain_block[:, :, :, 0, :], (0, 3, 1, 2))
    gain_im = jnp.transpose(gain_block[:, :, :, 1, :], (0, 3, 1, 2))
    rotated_re = gain_re * cosine - gain_im * sine_part
    rotated_im = gain_re * sine_part + gain_im * cosine
    return (cosine, sine_part, rotated_re, rotated_im)


def normal_terms(gains_full, tiles, vis, flags, station_uvw, src_lm, flux):
    item_count = tiles.shape[0]
    block_count = STATIONS // SB
    blocks = gains_full.reshape(block_count, SB, DIRS, 2, CHANS)
    row_block = tiles[:, 0]
    col_block = tiles[:, 1]
    step_index = tiles[:, 2]
    labels = jnp.arange(block_count, dtype=jnp.int32)
    pick_row = (row_block[:, None] == labels[None, :]).astype(jnp.float32)
    pick_col = (col_block[:, None] == labels[None, :]).astype(jnp.float32)
    positions = station_uvw[step_index].reshape(item_count, 3, block_count, SB)
    row_uvw = product("nb,nxbs->nxs", pick_row, positions)
    col_uvw = product("nb,nxbs->nxs", pick_col, positions)
    source_l = src_lm[0]
    source_m = src_lm[1]
    source_n = jnp.sqrt(1.0 - source_l * source_l - source_m * source_m) - 1.0
    frequency = 1.0 + jnp.arange(CHANS, dtype=jnp.float32) / CHANS
    row_cos, row_sin, row_re, row_im = rotate(
        row_uvw, blocks[row_block], source_l, source_m, source_n, frequency
    )
    col_cos, col_sin, col_re, col_im = rotate(
        col_uvw, blocks[col_block], source_l, source_m, source_n, frequency
    )
    flux_weight = jnp.transpose(flux)[None, :, None, :]
    scaled_re = row_re * flux_weight
    scaled_im = row_im * flux_weight
    col_stack = jnp.concatenate([col_re, col_im], axis=3)
    row_stack = jnp.concatenate([row_re, row_im], axis=3)
    model_rows = jnp.concatenate(
        [
            jnp.concatenate([scaled_re, scaled_im], axis=3),
            jnp.concatenate([scaled_im, -scaled_re], axis=3),
        ],
        axis=2,
    )
    model_both = product("nfrk,nfck->nfrc", model_rows, col_stack)
    model_re = model_both[:, :, :SB]
    model_im = model_both[:, :, SB:]
    row_local = jnp.arange(SB, dtype=jnp.int32)
    lower_part = (row_local[:, None] > row_local[None, :])[None, :, :]
    distinct = (row_block != col_block)[:, None, None]
    keep = jnp.logical_or(distinct, lower_part).astype(jnp.float32)
    baseline_mask = flags.reshape(item_count, SB, SB).astype(jnp.float32) * keep
    observed = vis.reshape(item_count, 2, CHANS, SB, SB)
    resid_re = (observed[:, 0].astype(jnp.float32) - model_re) * baseline_mask[:, None]
    resid_im = (observed[:, 1].astype(jnp.float32) - model_im) * baseline_mask[:, None]
    resid_stack = jnp.concatenate([resid_re, resid_im], axis=3)
    turned = jnp.concatenate(
        [jnp.concatenate([col_re, col_im], axis=3), jnp.concatenate([-col_im, col_re], axis=3)],
        axis=2,
    )
    srow = product("nfrc,nfck->nfrk", resid_stack, turned)
    srow_re = srow[..., :DIRS]
    srow_im = srow[..., DIRS:]
    cross = product("nfrc,nfrk->nfck", resid_stack, row_stack)
    scol_re = cross[:, :, :SB, :DIRS] + cross[:, :, SB:, DIRS:]
    scol_im = cross[:, :, :SB, DIRS:] - cross[:, :, SB:, :DIRS]
    nrow_re = flux_weight * (row_cos * srow_re + row_sin * srow_im)
    nrow_im = flux_weight * (row_cos * srow_im - row_sin * srow_re)
    ncol_re = flux_weight * (col_cos * scol_re + col_sin * scol_im)
    ncol_im = flux_weight * (col_cos * scol_im - col_sin * scol_re)
    flux_power = flux_weight * flux_weight
    drow = flux_power * product("nrc,nfck->nfrk", baseline_mask, col_re * col_re + col_im * col_im)
    dcol = flux_power * product("nrc,nfrk->nfck", baseline_mask, row_re * row_re + row_im * row_im)

    def deposit(row_term, col_term):
        summed = product("nb,nfrk->brkf", pick_row, row_term) + product(
            "nb,nfrk->brkf", pick_col, col_term
        )
        return summed.reshape(STATIONS * DIRS, CHANS)

    numerator = jnp.concatenate([deposit(nrow_re, ncol_re), deposit(nrow_im, ncol_im)], axis=1)
    denominator = deposit(drow, dcol)
    return (numerator, denominator)


def refine(current, numerator, denominator):
    return current + 0.5 * numerator / (jnp.concatenate([denominator, denominator], axis=1) + 1.0)


def on_device(gains, tiles, vis, flags, station_uvw, src_lm, flux):
    gathered = lax.all_gather(gains, "tile", axis=0, tiled=True)
    owned = gains
    for iteration in range(ITERS):
        numerator, denominator = normal_terms(
            gathered, tiles, vis, flags, station_uvw, src_lm, flux
        )
        num_share, den_share = (
            lax.psum_scatter(numerator, "tile", scatter_dimension=0, tiled=True),
            lax.psum_scatter(denominator, "tile", scatter_dimension=0, tiled=True),
        )
        owned = refine(owned, num_share, den_share)
        if iteration + 1 < ITERS:
            gathered = lax.all_gather(owned, "tile", axis=0, tiled=True)
    return owned


def solution(mesh):
    placed = (
        P(("group", "tile"), None),
        P(("group", "tile"), None),
        P(("group", "tile"), None, None, None),
        P(("group", "tile"), None),
        P("group", None, None),
        P(),
        P(),
    )
    return jax.shard_map(
        on_device, mesh=mesh, in_specs=placed, out_specs=P(("group", "tile"), None), check_vma=False
    )
```

profile of v0, /device:TPU:0, one launch (start us, length us, event | category | flops | bytes accessed | tf_op | source)
XLA Modules:
  0.0 947.9 jit_solution(11952612420806867049)
XLA Ops:
  32.0 30.9 %all-gather.3.cloned.1.call-done = f32[16384,64]{0,1:T(8,128)} async-done(((f32[1024,64]{0,1:T(8,128)}), f32[16384,64]{0,1:T(8,128)}) %all-gather.3.cloned.1.call-update) | async-done | bytes 4194320 | tf_op jit(solution)/shard_map/all_gather | solution.py:119
  62.9 10.8 %reshape.113 = f32[16,32,32,2,32]{2,1,0,4,3:T(8,128)} reshape(f32[16384,64]{0,1:T(8,128)} %all-gather.3.cloned.1.call-done) | data formatting | bytes 8388608 | tf_op jit(solution)/shard_map/reshape | solution.py:41
  73.6 18.3 %copy.56 = f32[16,32,32,2,32]{4,2,3,1,0:T(8,128)} copy(f32[16,32,32,2,32]{2,1,0,4,3:T(8,128)} %reshape.113) | data formatting | bytes 8388608 | tf_op jit(solution)/shard_map/reshape | solution.py:41
  92.0 10.1 %gather_fusion.2 = f32[8,32,32,2,32]{4,2,3,1,0:T(8,128)} fusion(f32[16,32,32,2,32]{4,2,3,1,0:T(8,128)} %copy.56, s32[1024]{0:T(1024)S(1)} %get-tuple-element.72), kind=kCustom, calls=%fused_computation.2 | custom fusion | bytes 4194336 | tf_op jit(solution)/shard_map/gather | solution.py:59
  102.1 10.1 %gather_fusion.1 = f32[8,32,32,2,32]{4,2,3,1,0:T(8,128)} fusion(f32[16,32,32,2,32]{4,2,3,1,0:T(8,128)} %copy.56, s32[1024]{0:T(1024)S(1)} %get-tuple-element.73), kind=kCustom, calls=%fused_computation.1 | custom fusion | bytes 4194336 | tf_op jit(solution)/shard_map/gather | solution.py:56
  112.2 8.2 fusion.220
  120.4 6.4 copy.114
  126.8 8.1 fusion.221
  154.0 36.1 %fusion.216 = (f32[8,32,32,32]{3,2,1,0:T(8,128)}, f32[8,32,32,32]{3,2,1,0:T(8,128)}, f32[8,32,32,32]{3,2,1,0:T(8,128)S(1)}, f32[8,32,32,32]{3,2,1,0:T(8,128)}, f...) fusion(f32[32,32]{1,0:T(8,128)S(1)} %copy.54, ...), kind=kLoop, calls=%fused_computation.247 | loop fusion | flops 4718592 | bytes 12652672 | tf_op jit(solution)/shard_map/neg | solution.py:69
  193.5 8.5 multiply_bitcast_fusion.2
  207.6 10.7 %multiply_bitcast_fusion.3 = f32[8,32,32,32]{2,3,1,0:T(8,128)} fusion(f32[8,32,32,32]{3,2,1,0:T(8,128)} %get-tuple-element.71, f32[8,32,32,32]{3,2,1,0:T(8,128)} %get-tuple-element.69, f32[32,32]{1,0:T(8,128)S(1)} %copy.72, f32[8,32,32]{2,1,0:T(8,128)S(1)} %or_select_fusion), kind=kOutput, calls=%fused_computation.164 | convolution fusion | flops 101711872 | bytes 3182592 | tf_op jit(solution)/shard_map/nrc,nfck->nfrk/dot_general | solution.py:19
  234.3 6.8 copy.77
  241.1 7.2 reshape.116
  248.4 20.7 %fusion = f32[8,32,64,32]{2,3,1,0:T(8,128)S(1)} fusion(f32[8,32,32,32]{3,2,1,0:T(8,128)} %get-tuple-element.16, f32[8,32,32,32]{3,2,1,0:T(8,128)} %get-tuple-element.25, f32[8,32,32,32]{3,2,1,0:T(8,128)} %get-tuple-element.17, f32[8,32,32,32]{3,2,1,0:T(8,128)} %get-tuple-element.71, f32[8,32,32,32]{3,2,1,0:T(8,128)} %get-tuple-element.69), kind=kOutput, calls=%fused_computation.5 | convolution fusion | flops 406323200 | bytes 7340032 | tf_op jit(solution)/shard_map/nfrk,nfck->nfrc/dot_general | solution.py:19
  274.2 13.7 %fusion.33 = f32[8,32,64,64]{3,2,1,0:T(8,128)} fusion(f32[8,32,32,32]{2,3,1,0:T(8,128)} %get-tuple-element.44, f32[8,32,32,32]{2,3,1,0:T(8,128)} %get-tuple-element.43, f32[8,32,32,32]{3,2,1,0:T(8,128)} %copy-done.6, f32[8,32,32,32]{3,2,1,0:T(8,128)S(1)} %copy-done.5), kind=kOutput, calls=%fused_computation.46 | convolution fusion | flops 403701760 | bytes 8388608 | tf_op jit(solution)/shard_map/nfrc,nfrk->nfck/dot_general | solution.py:19
  287.9 21.4 %fusion.8 = f32[8,32,32,64]{3,2,1,0:T(8,128)} fusion(f32[8,32,32,32]{3,2,1,0:T(8,128)S(1)} %copy-done.2, f32[8,32,32,32]{3,2,1,0:T(8,128)} %get-tuple-element.70, f32[8,32,32,32]{3,2,1,0:T(8,128)} %get-tuple-element.71, f32[8,32,32,32]{2,3,1,0:T(8,128)} %get-tuple-element.44, f32[8,32,32,32]{2,3,1,0:T(8,128)} %get-tuple-element.43), kind=kOutput, calls=%fused_computation.14 | convolution fusion | flops 406323200 | bytes 7340032 | tf_op jit(solution)/shard_map/nfrc,nfck->nfrk/dot_general | solution.py:19
  309.3 36.6 %fusion.73 = (f32[8,32,32,32]{3,2,1,0:T(8,128)}, f32[8,32,32,32]{3,2,1,0:T(8,128)S(1)}, f32[8,32,32,32]{3,2,1,0:T(8,128)S(1)}, f32[8,32,32,32]{3,2,1,0:T(8,128)}) fusion(f32[8,32,32,64]{3,2,1,0:T(8,128)} %fusion.8, f32[32]{0:T(128)S(1)} %multiply_add_fusion, f32[8,32,32]{2,1,0:T(8,128)S(1)} %get-tuple-element.62, f32[32,32]{1,0:T(8,128)S(1)} %copy.54, ...), kind=kLoop, calls=%fused_computation.94 | loop fusion | flops 5242880 | bytes 10555520 | tf_op jit(solution)/shard_map/mul | solution.py:95
  357.8 7.2 copy.71
  365.0 7.2 reshape.115
  372.2 8.2 fusion.118
  386.5 6.8 copy.68
  393.3 7.2 reshape.114
  405.1 71.2 %reduce-scatter.5.cloned.1.call-done = f32[1024,64]{0,1:T(8,128)} async-done(((f32[16384,64]{0,1:T(8,128)}), f32[1024,64]{0,1:T(8,128)}) %reduce-scatter.5.cloned.1.call-update) | async-done | bytes 262160 | tf_op jit(solution)/shard_map/reduce_scatter | solution.py:126
  478.2 49.7 %all-gather.5.cloned.1.call-done = f32[16384,64]{0,1:T(8,128)} async-done(((f32[1024,64]{0,1:T(8,128)}), f32[16384,64]{0,1:T(8,128)}) %all-gather.5.cloned.1.call-update) | async-done | bytes 4194320 | tf_op jit(solution)/shard_map/all_gather | solution.py:131
  527.9 11.0 %reshape.117 = f32[16,32,32,2,32]{2,1,0,4,3:T(8,128)} reshape(f32[16384,64]{0,1:T(8,128)} %all-gather.5.cloned.1.call-done) | data formatting | bytes 8388608 | tf_op jit(solution)/shard_map/reshape | solution.py:41
  538.9 18.3 %copy.78 = f32[16,32,32,2,32]{4,2,3,1,0:T(8,128)} copy(f32[16,32,32,2,32]{2,1,0,4,3:T(8,128)} %reshape.117) | data formatting | bytes 8388608 | tf_op jit(solution)/shard_map/reshape | solution.py:41
  557.2 10.3 %gather_fusion.4 = f32[8,32,32,2,32]{4,2,3,1,0:T(8,128)} fusion(f32[16,32,32,2,32]{4,2,3,1,0:T(8,128)} %copy.78, s32[1024]{0:T(1024)} %copy-done.25), kind=kCustom, calls=%fused_computation.4 | custom fusion | bytes 4194336 | tf_op jit(solution)/shard_map/gather | solution.py:59
  567.5 10.2 %gather_fusion.3 = f32[8,32,32,2,32]{4,2,3,1,0:T(8,128)} fusion(f32[16,32,32,2,32]{4,2,3,1,0:T(8,128)} %copy.78, s32[1024]{0:T(1024)} %copy-done.24), kind=kCustom, calls=%fused_computation.3 | custom fusion | bytes 4194336 | tf_op jit(solution)/shard_map/gather | solution.py:56
  577.7 8.1 fusion.218
  585.8 6.4 copy.119
  592.2 8.2 fusion.219
  600.3 6.4 copy.121
  606.8 6.4 copy.122
  619.6 36.3 %fusion.211 = (f32[8,32,32,32]{3,2,1,0:T(8,128)}, f32[8,32,32,32]{3,2,1,0:T(8,128)}, f32[8,32,32,32]{3,2,1,0:T(8,128)}, f32[8,32,32,32]{3,2,1,0:T(8,128)}, f32[8...) fusion(f32[32,32]{1,0:T(8,128)S(1)} %copy.54, ...), kind=kLoop, calls=%fused_computation.245 | loop fusion | flops 4718592 | bytes 12652672 | tf_op jit(solution)/shard_map/neg | solution.py:69
  655.9 9.0 multiply_bitcast_fusion.1
  664.8 21.1 %fusion.16 = f32[8,32,64,32]{2,3,1,0:T(8,128)} fusion(f32[8,32,32,32]{3,2,1,0:T(8,128)} %get-tuple-element.9, f32[8,32,32,32]{3,2,1,0:T(8,128)} %get-tuple-element.21, f32[8,32,32,32]{3,2,1,0:T(8,128)} %get-tuple-element.10, f32[8,32,32,32]{3,2,1,0:T(8,128)S(1)} %get-tuple-element.68, f32[8,32,32,32]{3,2,1,0:T(8,128)S(1)} %get-tuple-element.66), kind=kOutput, calls=%fused_computation.22 | convolution fusion | flops 406323200 | bytes 7340032 | tf_op jit(solution)/shard_map/nfrk,nfck->nfrc/dot_general | solution.py:19
  686.0 8.1 fusion.67
  694.1 10.3 %multiply_bitcast_fusion = f32[8,32,32,32]{2,3,1,0:T(8,128)} fusion(f32[8,32,32,32]{3,2,1,0:T(8,128)} %get-tuple-element.22, f32[8,32,32,32]{3,2,1,0:T(8,128)S(1)} %copy-done.7, f32[32,32]{1,0:T(8,128)S(1)} %copy-done.23, f32[8,32,32]{2,1,0:T(8,128)S(1)} %copy-done.16), kind=kOutput, calls=%fused_computation.149 | convolution fusion | flops 101711872 | bytes 3182592 | tf_op jit(solution)/shard_map/nrc,nfrk->nfck/dot_general | solution.py:19
  704.4 11.9 %fusion.32 = f32[8,32,64,64]{3,2,1,0:T(8,128)} fusion(f32[8,32,32,32]{2,3,1,0:T(8,128)} %get-tuple-element.42, f32[8,32,32,32]{2,3,1,0:T(8,128)} %get-tuple-element.41, f32[8,32,32,32]{3,2,1,0:T(8,128)S(1)} %copy-done.8, f32[8,32,32,32]{3,2,1,0:T(8,128)S(1)} %copy-done.7), kind=kOutput, calls=%fused_computation.45 | convolution fusion | flops 403701760 | bytes 8388608 | tf_op jit(solution)/shard_map/nfrc,nfrk->nfck/dot_general | solution.py:19
  716.3 21.5 %fusion.24 = f32[8,32,32,64]{3,2,1,0:T(8,128)} fusion(f32[8,32,32,32]{3,2,1,0:T(8,128)S(1)} %get-tuple-element.66, f32[8,32,32,32]{3,2,1,0:T(8,128)} %get-tuple-element.67, f32[8,32,32,32]{3,2,1,0:T(8,128)} %copy-done.3, f32[8,32,32,32]{2,3,1,0:T(8,128)} %get-tuple-element.42, f32[8,32,32,32]{2,3,1,0:T(8,128)} %get-tuple-element.41), kind=kOutput, calls=%fused_computation.31 | convolution fusion | flops 406323200 | bytes 7340032 | tf_op jit(solution)/shard_map/nfrc,nfck->nfrk/dot_general | solution.py:19
  759.6 6.7 copy.96
  766.4 7.3 reshape.120
  773.7 36.5 %fusion.79 = (f32[8,32,32,32]{3,2,1,0:T(8,128)}, f32[8,32,32,32]{3,2,1,0:T(8,128)S(1)}, f32[8,32,32,32]{3,2,1,0:T(8,128)S(1)}, f32[8,32,32,32]{3,2,1,0:T(8,128)}) fusion(f32[8,32,32,64]{3,2,1,0:T(8,128)} %fusion.24, f32[32]{0:T(128)S(1)} %multiply_add_fusion, f32[8,32,32]{2,1,0:T(8,128)S(1)} %get-tuple-element.62, f32[32,32]{1,0:T(8,128)S(1)} %copy.54, ...), kind=kLoop, calls=%fused_computation.100 | loop fusion | flops 5242880 | bytes 10555520 | tf_op jit(solution)/shard_map/mul | solution.py:95
  822.1 7.0 copy.91
  835.4 8.3 fusion.110
  849.8 6.8 copy.88
  856.6 7.2 reshape.118
  867.7 71.0 %reduce-scatter.9.cloned.1.call-done = f32[1024,64]{0,1:T(8,128)} async-done(((f32[16384,64]{0,1:T(8,128)}), f32[1024,64]{0,1:T(8,128)}) %reduce-scatter.9.cloned.1.call-update) | async-done | bytes 262160 | tf_op jit(solution)/shard_map/reduce_scatter | solution.py:126
  (121 shorter events, 157.3 us)
Async XLA Ops:
  6.5 5.0 copy-start
  6.5 56.3 %all-gather.3.cloned.1.call-start = ((), (), s32[]{:S(2)}) async-start(), calls=%async_computation.4 | async-start | bytes 4456448 | tf_op jit(solution)/shard_map/all_gather | solution.py:119
  7.3 397.8 %reduce-scatter.7.cloned.1.call-start = ((), (), s32[]{:S(2)}) async-start(), calls=%async_computation.6 | async-start | bytes 2228224 | tf_op jit(solution)/shard_map/reduce_scatter | solution.py:127
  8.9 198.7 %copy-start.22 = (f32[32,32]{1,0:T(8,128)}, f32[32,32]{1,0:T(8,128)S(1)}, u32[]{:S(2)}) copy-start(f32[32,32]{1,0:T(8,128)S(1)} %copy.72) | copy-start | bytes 12292
  10.6 197.0 %copy-start.15 = (f32[8,32,32]{2,1,0:T(8,128)}, f32[8,32,32]{2,1,0:T(8,128)S(1)}, u32[]{:S(2)}) copy-start(f32[8,32,32]{2,1,0:T(8,128)S(1)} %or_select_fusion) | copy-start | bytes 98308
  10.7 258.3 %copy-start.20 = (f32[8,32,32]{1,2,0:T(8,128)}, f32[8,32,32]{1,2,0:T(8,128)S(1)}, u32[]{:S(2)}) copy-start(f32[8,32,32]{1,2,0:T(8,128)S(1)} %copy.62) | copy-start | bytes 98308
  24.4 7.2 copy-start.26
  31.6 60.4 %copy-start.25 = (s32[1024]{0:T(1024)}, s32[1024]{0:T(1024)S(1)}, u32[]{:S(2)}) copy-start(s32[1024]{0:T(1024)S(1)} %get-tuple-element.72) | copy-start | bytes 12292
  31.6 70.5 %copy-start.24 = (s32[1024]{0:T(1024)}, s32[1024]{0:T(1024)S(1)}, u32[]{:S(2)}) copy-start(s32[1024]{0:T(1024)S(1)} %get-tuple-element.73) | copy-start | bytes 12292
  31.9 277.4 %copy-start.17 = (f32[8,32,32]{2,1,0:T(8,128)}, f32[8,32,32]{2,1,0:T(8,128)S(1)}, u32[]{:S(2)}) copy-start(f32[8,32,32]{2,1,0:T(8,128)S(1)} %get-tuple-element.63) | copy-start | bytes 98308
  190.2 2.0 copy-start.4
  190.2 3.3 copy-start.6
  224.0 6.2 copy-start.11
  248.3 227.9 %reduce-scatter.5.cloned.1.call-start = ((), (), s32[]{:S(2)}) async-start(), calls=%async_computation.5 | async-start | bytes 4456448 | tf_op jit(solution)/shard_map/reduce_scatter | solution.py:126
  248.4 20.7 %copy-start.9 = (bf16[8,1,32,32,32]{3,4,2,0,1:T(8,128)(2,1)S(1)}, bf16[8,1,32,32,32]{3,4,2,0,1:T(8,128)(2,1)}, u32[]{:S(2)}) copy-start(bf16[8,1,32,32,32]{3,4,2,0,1:T(8,128)(2,1)} %copy.118) | copy-start | bytes 1572868
  269.1 5.1 copy-start.5
  274.2 13.7 %copy-start.2 = (f32[8,32,32,32]{3,2,1,0:T(8,128)S(1)}, f32[8,32,32,32]{3,2,1,0:T(8,128)}, u32[]{:S(2)}) copy-start(f32[8,32,32,32]{3,2,1,0:T(8,128)} %get-tuple-element.69) | copy-start | bytes 3145732
  372.2 8.2 copy-start.14
  405.0 71.3 %copy-start.21 = (f32[1024,64]{0,1:T(8,128)S(1)}, f32[1024,64]{0,1:T(8,128)}, u32[]{:S(2)}) copy-start(f32[1024,64]{0,1:T(8,128)} %param.7) | copy-start | bytes 786436
  405.0 122.9 %all-gather.5.cloned.1.call-start = ((), (), s32[]{:S(2)}) async-start(), calls=%async_computation.7 | async-start | bytes 4456448 | tf_op jit(solution)/shard_map/all_gather | solution.py:131
  478.1 389.6 %reduce-scatter.11.cloned.1.call-start = ((), (), s32[]{:S(2)}) async-start(), calls=%async_computation.9 | async-start | bytes 2228224 | tf_op jit(solution)/shard_map/reduce_scatter | solution.py:127
  619.5 36.3 %copy-start.16 = (f32[8,32,32]{2,1,0:T(8,128)S(1)}, f32[8,32,32]{2,1,0:T(8,128)}, u32[]{:S(2)}) copy-start(f32[8,32,32]{2,1,0:T(8,128)} %copy-done.15) | copy-start | bytes 98308
  619.6 36.3 %copy-start.23 = (f32[32,32]{1,0:T(8,128)S(1)}, f32[32,32]{1,0:T(8,128)}, u32[]{:S(2)}) copy-start(f32[32,32]{1,0:T(8,128)} %copy-done.22) | copy-start | bytes 12292
  655.8 9.0 copy-start.3
  664.8 21.1 %copy-start.10 = (bf16[8,1,32,32,32]{3,4,2,0,1:T(8,128)(2,1)S(1)}, bf16[8,1,32,32,32]{3,4,2,0,1:T(8,128)(2,1)}, u32[]{:S(2)}) copy-start(bf16[8,1,32,32,32]{3,4,2,0,1:T(8,128)(2,1)} %copy.118) | copy-start | bytes 1572868
  686.0 8.1 copy-start.7
  694.1 10.3 %copy-start.8 = (f32[8,32,32,32]{3,2,1,0:T(8,128)S(1)}, f32[8,32,32,32]{3,2,1,0:T(8,128)}, u32[]{:S(2)}) copy-start(f32[8,32,32,32]{3,2,1,0:T(8,128)} %get-tuple-element.22) | copy-start | bytes 3145732
  749.1 6.4 copy-start.12
  766.3 7.3 copy-start.18
  773.6 165.1 %reduce-scatter.9.cloned.1.call-start = ((), (), s32[]{:S(2)}) async-start(), calls=%async_computation.8 | async-start | bytes 4456448 | tf_op jit(solution)/shard_map/reduce_scatter | solution.py:126
  835.4 8.3 copy-start.13
  863.8 76.8 %copy-start.1 = (f32[16,3,512]{2,0,1:T(8,128)S(1)}, f32[16,3,512]{2,0,1:T(8,128)}, u32[]{:S(2)}) copy-start(f32[16,3,512]{2,0,1:T(8,128)} %param.11) | copy-start | bytes 294916
  867.7 71.1 %copy-start.19 = (f32[1024,64]{0,1:T(8,128)S(1)}, f32[1024,64]{0,1:T(8,128)}, u32[]{:S(2)}) copy-start(f32[1024,64]{0,1:T(8,128)} %fusion.155) | copy-start | bytes 786436
Sparse Core Ops, SparseCore 0:
  9.5 53.2 all-gather.2
  248.4 60.0 reduce-scatter.6
  405.1 71.0 reduce-scatter.4
  478.3 49.5 all-gather.4
  773.8 60.0 reduce-scatter.10
  867.8 70.8 reduce-scatter.8
where the time goes:
time: 959 us; the launch traced here: 948 us
  local copies, waits for them, and re-layouts  313 us (33%)
  waiting for transfers between devices  224 us (23%)
  matrix products  223 us (23%)
  other arithmetic  174 us (18%)
  between operations  14.4 us (2%)
    dot_general x24, matrix products, product(): return jnp.einsum(form, left, right, precision=highest)  223 us
    reduce_scatter x2, waiting for transfers between devices, on_device(): lax.psum_scatter(numerator, 'tile', scatter_dimension=0, tiled=True)  142 us
    mul x2, other arithmetic, normal_terms(): nrow_re = flux_weight * (row_cos * srow_re + row_sin * srow_im)  73.1 us
    neg x2, other arithmetic, normal_terms(): -scaled_re  72.4 us
    unnamed x64, local copies, waits for them, and re-layouts  61.7 us
    reshape x4, local copies, waits for them, and re-layouts, normal_terms(): blocks = gains_full.reshape(block_count, SB, DIRS, 2, CHANS)  58.4 us
    all_gather x1, waiting for transfers between devices, on_device(): gathered = lax.all_gather(owned, 'tile', axis=0, tiled=True)  49.7 us
    reshape x6, local copies, waits for them, and re-layouts, deposit(): return summed.reshape(STATIONS * DIRS, CHANS)  42.4 us
  transfers between devices with their start and end apart: 6, of which 4 were waited for; matrix products, arithmetic and copies ran while one was open for 29% of the time, Pallas kernels for 0%

commit v1 on v0

v1 whole, which is shorter than its diff:
```python
import functools
import math

import jax
import jax.numpy as jnp
from jax import lax
from jax.experimental import pallas as pl
from jax.experimental.pallas import tpu as pltpu
from jax.sharding import PartitionSpec as P

SB = 32
ITERS = 2
GROUPS = 2
LANES = 128
VMEM = 40 * 1024 * 1024

highest = lax.Precision.HIGHEST


def series(first, step, terms):
    out = []
    for j in range(terms):
        degree = first + step * j
        out.append((-1.0) ** j * math.pi**degree / math.factorial(degree))
    return out


SIN = series(1, 2, 7)
COS = series(0, 2, 7)


def horner(coefficients, z):
    total = jnp.full_like(z, coefficients[-1])
    for value in reversed(coefficients[:-1]):
        total = total * z + value
    return total


def phasor_kernel(tiles_ref, uvw_ref, lanes_ref, cos_ref, sin_ref):
    uvw = uvw_ref[0, 0]
    u, v, w = uvw[:, 0:1], uvw[:, 1:2], uvw[:, 2:3]
    width = lanes_ref.shape[1]
    for start in range(0, width, 256):
        cut = slice(start, start + 256)
        delay = u * lanes_ref[0:1, cut] + v * lanes_ref[1:2, cut] + w * lanes_ref[2:3, cut]
        turns = delay * lanes_ref[3:4, cut]
        r = turns - jnp.floor(turns + 0.5)
        z = r * r
        s = r * horner(SIN, z)
        c = horner(COS, z)
        cos_ref[0, :, cut] = 1.0 - 2.0 * s * s
        sin_ref[0, :, cut] = 2.0 * s * c


def phasors(tiles, uvw_columns, lane_rows):
    items = tiles.shape[0]
    width = lane_rows.shape[1]

    def pick(i, t):
        return (t[i // 2, 2], t[i // 2, i % 2], 0, 0)

    shape = jax.ShapeDtypeStruct((2 * items, SB, width), jnp.float32)
    block = pl.BlockSpec((1, SB, width), lambda i, t: (i, 0, 0))
    return pl.pallas_call(
        phasor_kernel,
        grid_spec=pltpu.PrefetchScalarGridSpec(
            num_scalar_prefetch=1,
            grid=(2 * items,),
            in_specs=[
                pl.BlockSpec((1, 1, SB, 3), pick),
                pl.BlockSpec((8, width), lambda i, t: (0, 0)),
            ],
            out_specs=[block, block],
        ),
        out_shape=[shape, shape],
        compiler_params=pltpu.CompilerParams(vmem_limit_bytes=VMEM),
        cost_estimate=pl.CostEstimate(
            flops=2 * items * SB * width * 40,
            bytes_accessed=2 * items * SB * width * 8,
            transcendentals=0,
        ),
    )(tiles, uvw_columns, lane_rows)


def split(x):
    high = x.astype(jnp.bfloat16)
    return high, (x - high.astype(jnp.float32)).astype(jnp.bfloat16)


def dot(left, right, left_dim, right_dim):
    def one(a, b):
        return lax.dot_general(
            a,
            b,
            (((left_dim,), (right_dim,)), ((), ())),
            preferred_element_type=jnp.float32,
        )

    return one(left[0], right[0]) + (one(left[0], right[1]) + one(left[1], right[0]))


def normal_kernel(
    tiles_ref, grow_ref, gcol_ref, cos_ref, sin_ref, vis_ref, w_ref, flux_ref, out_ref
):
    item = pl.program_id(0)

    @pl.when(item == 0)
    def _():
        out_ref[...] = jnp.zeros_like(out_ref)

    width = flux_ref.shape[1]
    row_block = tiles_ref[item, 0]
    col_block = tiles_ref[item, 1]
    weights = jnp.concatenate([w_ref[0]] * 4, axis=0)
    own = (
        lax.broadcasted_iota(jnp.int32, (LANES, LANES), 0) // SB
        == lax.broadcasted_iota(jnp.int32, (LANES, LANES), 1) // SB
    )
    mask = own.astype(jnp.float32)
    mask_half = mask.astype(jnp.bfloat16)
    for start in range(0, width, LANES):
        re = slice(start, start + LANES)
        im = slice(width + start, width + start + LANES)
        flux = flux_ref[:, re]
        cr, sr = cos_ref[0, :, re], sin_ref[0, :, re]
        cc, sc = cos_ref[1, :, re], sin_ref[1, :, re]
        a_re, a_im = grow_ref[0, :, re], grow_ref[0, :, im]
        b_re, b_im = gcol_ref[0, :, re], gcol_ref[0, :, im]
        row_re, row_im = split(a_re * cr - a_im * sr), split(a_re * sr + a_im * cr)
        col_re = split(flux * (b_re * cc - b_im * sc))
        col_im = split(flux * (b_re * sc + b_im * cc))
        rows = [
            jnp.concatenate(
                [
                    jnp.concatenate([row_re[j]] * 4, axis=0) * mask_half,
                    jnp.concatenate([row_im[j]] * 4, axis=0) * mask_half,
                ],
                axis=1,
            )
            for j in range(2)
        ]
        cols = [
            jnp.concatenate(
                [
                    jnp.concatenate([col_re[j], col_im[j]], axis=1),
                    jnp.concatenate([-col_im[j], col_re[j]], axis=1),
                ],
                axis=0,
            )
            for j in range(2)
        ]
        model = dot(rows, cols, 1, 1)
        observed = vis_ref[0, start : start + LANES, :].astype(jnp.float32)
        resid = split((observed - model) * weights)
        srow = dot(resid, cols, 1, 0)
        cross = dot(resid, rows, 0, 0)
        s_re, s_im = srow[:, :LANES] * mask, srow[:, LANES:] * mask
        s_re = (s_re[0:32] + s_re[32:64]) + (s_re[64:96] + s_re[96:128])
        s_im = (s_im[0:32] + s_im[32:64]) + (s_im[64:96] + s_im[96:128])
        t_re = flux * (cross[:SB, :LANES] + cross[SB:, LANES:])
        t_im = flux * (cross[:SB, LANES:] - cross[SB:, :LANES])
        out_ref[row_block, :, re] += cr * s_re + sr * s_im
        out_ref[row_block, :, im] += cr * s_im - sr * s_re
        out_ref[col_block, :, re] += cc * t_re + sc * t_im
        out_ref[col_block, :, im] += cc * t_im - sc * t_re


def normal_terms(group, tiles, gathered, cosine, sine_part, vis_rows, weights, flux_row):
    items = tiles.shape[0]
    width = flux_row.shape[1]
    blocks = gathered.shape[0]
    gain_spec = lambda side: pl.BlockSpec(
        (1, SB, 2 * width), lambda i, t: (t[i, side], 0, 0)
    )
    turn_spec = pl.BlockSpec((2, SB, width), lambda i, t: (i, 0, group))
    return pl.pallas_call(
        normal_kernel,
        grid_spec=pltpu.PrefetchScalarGridSpec(
            num_scalar_prefetch=1,
            grid=(items,),
            in_specs=[
                gain_spec(0),
                gain_spec(1),
                turn_spec,
                turn_spec,
                pl.BlockSpec((1, width, 2 * SB), lambda i, t: (i, group, 0)),
                pl.BlockSpec((1, SB, 2 * SB), lambda i, t: (i, 0, 0)),
                pl.BlockSpec((1, width), lambda i, t: (0, 0)),
            ],
            out_specs=pl.BlockSpec((blocks, SB, 2 * width), lambda i, t: (0, 0, 0)),
        ),
        out_shape=jax.ShapeDtypeStruct((blocks, SB, 2 * width), jnp.float32),
        compiler_params=pltpu.CompilerParams(vmem_limit_bytes=VMEM),
        cost_estimate=pl.CostEstimate(
            flops=items * width * 3 * 8 * SB * SB * 24,
            bytes_accessed=items * width * SB * 30 + blocks * SB * width * 8,
            transcendentals=0,
        ),
    )(tiles, gathered, gathered, cosine, sine_part, vis_rows, weights, flux_row)


def on_device(gains, tiles, vis, flags, station_uvw, src_lm, flux):
    dirs, chans = flux.shape
    times, _, stations = station_uvw.shape
    items = tiles.shape[0]
    blocks = stations // SB
    owned_count = gains.shape[0] // dirs
    per = chans // GROUPS
    width = per * dirs

    turned = gains.reshape(owned_count, dirs, 2, GROUPS, per).transpose(3, 0, 2, 4, 1)
    owned = [turned[g].reshape(owned_count, 2 * width) for g in range(GROUPS)]

    def gather(x):
        return lax.all_gather(x, "tile", axis=0, tiled=True)

    gathered = [gather(x) for x in owned]

    keep = jnp.logical_or(
        (tiles[:, 0] != tiles[:, 1])[:, None],
        (jnp.arange(SB)[:, None] > jnp.arange(SB)[None, :]).reshape(1, SB * SB),
    )
    weights = jnp.where(keep, flags, 0).astype(jnp.float32)
    all_weights = gather(weights)
    all_tiles = gather(tiles)

    source_l, source_m = src_lm[0], src_lm[1]
    squares = source_l * source_l + source_m * source_m
    source_n = -squares / (1.0 + jnp.sqrt(1.0 - squares))
    frequency = 1.0 + jnp.arange(chans, dtype=jnp.float32) / chans
    lane_rows = jnp.stack(
        [jnp.tile(source_l, chans), jnp.tile(source_m, chans), jnp.tile(source_n, chans)]
        + [jnp.repeat(frequency, dirs)] * 5
    )
    uvw_columns = station_uvw.reshape(times, 3, blocks, SB).transpose(0, 2, 3, 1)
    cosine, sine_part = phasors(tiles, uvw_columns, lane_rows)

    vis_rows = vis.reshape(items, 2, chans, SB, SB).transpose(0, 2, 3, 1, 4)
    vis_rows = vis_rows.reshape(items, chans * SB, 2 * SB)
    square = weights.reshape(items, SB, SB)
    pair_weights = jnp.concatenate([square, square], axis=2)
    flux_rows = flux.T.reshape(GROUPS, 1, width)

    first = lax.axis_index("tile") * owned_count
    block, offset = first // SB, first % SB
    labels = jnp.arange(blocks, dtype=jnp.int32)[None, :]
    is_row = (all_tiles[:, 0:1] == block) & (all_tiles[:, 1:2] == labels)
    is_col = (all_tiles[:, 1:2] == block) & (all_tiles[:, 0:1] == labels)
    as_row = jnp.einsum(
        "ib,ix->bx", is_row.astype(jnp.float32), all_weights, precision=highest
    ).reshape(blocks, SB, SB)
    as_col = jnp.einsum(
        "ib,ix->bx", is_col.astype(jnp.float32), all_weights, precision=highest
    ).reshape(blocks, SB, SB)
    as_row = lax.dynamic_slice_in_dim(as_row, offset, owned_count, 1)
    as_col = lax.dynamic_slice_in_dim(as_col, offset, owned_count, 2)
    pair_counts = (as_row.transpose(1, 0, 2) + as_col.transpose(2, 0, 1)).reshape(
        owned_count, stations
    )

    for iteration in range(ITERS):
        updated = []
        for g in range(GROUPS):
            full = gathered[g]
            numerator = normal_terms(
                g,
                tiles,
                full.reshape(blocks, SB, 2 * width),
                cosine,
                sine_part,
                vis_rows,
                pair_weights,
                flux_rows[g],
            ).reshape(stations, 2 * width)
            share = lax.psum_scatter(numerator, "tile", scatter_dimension=0, tiled=True)
            power = full[:, :width] * full[:, :width] + full[:, width:] * full[:, width:]
            denominator = (flux_rows[g] * flux_rows[g]) * jnp.dot(
                pair_counts, power, precision=highest
            )
            scale = 0.5 / (denominator + 1.0)
            updated.append(owned[g] + share * jnp.concatenate([scale, scale], axis=1))
        owned = updated
        if iteration + 1 < ITERS:
            gathered = [gather(x) for x in owned]

    stacked = jnp.stack(owned).reshape(GROUPS, owned_count, 2, per, dirs)
    return stacked.transpose(1, 4, 2, 0, 3).reshape(owned_count * dirs, 2 * chans)


def solution(mesh):
    placed = (
        P(("group", "tile"), None),
        P(("group", "tile"), None),
        P(("group", "tile"), None, None, None),
        P(("group", "tile"), None),
        P("group", None, None),
        P(),
        P(),
    )
    return jax.shard_map(
        on_device, mesh=mesh, in_specs=placed, out_specs=P(("group", "tile"), None), check_vma=False
    )
```

time: 959 us -> 451 us (0.47); the launches traced: 948 us -> 450 us
  local copies, waits for them, and re-layouts: 313 us -> 61.8 us
  matrix products: 223 us -> 8.76 us
  other arithmetic: 174 us -> 6.11 us
  waiting for transfers between devices: 224 us -> 272 us
  Pallas kernels: 0 us -> 47.5 us
  blocking collectives: 0 us -> 39.2 us
    dot_general x24 -> x6, matrix products: 223 us -> 8.76 us  [the longest x4 8.08 us: on_device(): jnp.dot(pair_counts, power, precision=highest)]
    mul x7 -> x1, other arithmetic: 87.3 us -> 0.61 us  [on_device(): flux_rows[g] * flux_rows[g]]
    reshape x12, local copies, waits for them, and re-layouts: 107 us -> 24.3 us  [the longest x2 13.3 us: on_device(): vis_rows = vis.reshape(items, 2, chans, SB, SB).transpose(0, 2, 3, 1, 4)]
    neg x2 -> x0, other arithmetic: 72.4 us -> none  [normal_terms(): -scaled_re]
    pallas_call x0 -> x5, Pallas kernels: none -> 47.5 us  [the longest x4 42.7 us: normal_terms(): pl.pallas_call(normal_kernel, grid_spec=pltpu.PrefetchScalarGridSpec(num_...]
    gather x5 -> x0, local copies, waits for them, and re-layouts: 41.4 us -> none  [the longest x2 20.4 us: normal_terms(): blocks[col_block]]
    add x6 -> x0, local copies, waits for them, and re-layouts: 41.1 us -> none  [deposit(): product('nb,nfrk->brkf', pick_row, row_term)]
    all_gather x0 -> x2, blocking collectives: none -> 39.2 us  [gather(): return lax.all_gather(x, 'tile', axis=0, tiled=True)]
  transfers between devices with their start and end apart: 6 -> 8, of which waited for: 4 -> 8; matrix products, arithmetic and copies ran while one was open for 29% -> 9% of each run, Pallas kernels for 0% -> 11%
where the time goes in v1:
time: 451 us; the launch traced here: 450 us
  waiting for transfers between devices  272 us (60%)
  local copies, waits for them, and re-layouts  61.8 us (14%)
  Pallas kernels  47.5 us (11%)
  blocking collectives  39.2 us (9%)
  between operations  13.9 us (3%)
  matrix products  8.76 us (2%)
  other arithmetic  6.11 us (1%)
    reduce_scatter x4, waiting for transfers between devices, on_device(): share = lax.psum_scatter(numerator, 'tile', scatter_dimension=0, tiled=True)  173 us
    all_gather x4, waiting for transfers between devices, gather(): return lax.all_gather(x, 'tile', axis=0, tiled=True)  98.9 us
    pallas_call x4, Pallas kernels, normal_terms(): pl.pallas_call(normal_kernel, grid_spec=pltpu.PrefetchScalarGridSpec(num_...  42.7 us
    all_gather x2, blocking collectives, gather(): return lax.all_gather(x, 'tile', axis=0, tiled=True)  39.2 us
    unnamed x70, local copies, waits for them, and re-layouts  33.8 us
    reshape x2, local copies, waits for them, and re-layouts, on_device(): vis_rows = vis.reshape(items, 2, chans, SB, SB).transpose(0, 2, 3, 1, 4)  13.3 us
  transfers between devices with their start and end apart: 8, of which 8 were waited for; matrix products, arithmetic and copies ran while one was open for 9% of the time, Pallas kernels for 11%

profile of v1, /device:TPU:0, one launch (start us, length us, event | category | flops | bytes accessed | tf_op | source)
XLA Modules:
  0.0 449.6 jit_solution(10886291386357307741)
XLA Ops:
  6.5 1.3 reshape.92
  12.1 4.3 reshape.95
  16.4 9.0 %copy.63 = bf16[8,2,32,32,32]{3,2,4,1,0:T(8,128)(2,1)} copy(bf16[8,2,32,32,32]{4,3,2,1,0:T(8,128)(2,1)} %reshape.95) | data formatting | bytes 2097152 | tf_op jit(solution)/shard_map/reshape | solution.py:238
  25.5 6.2 %reshape.96 = bf16[8,1024,64]{1,2,0:T(8,128)(2,1)S(1)} reshape(bf16[8,32,32,2,32]{2,1,4,3,0:T(8,128)(2,1)} %bitcast.76) | data formatting | bytes 2097152 | tf_op jit(solution)/shard_map/reshape | solution.py:239
  31.6 1.1 copy.66.vis_ref
  32.7 2.7 copy.61
  35.5 2.4 copy-done.10
  37.9 4.9 %shard_map.73 = (f32[16,32,1024]{2,1,0:T(8,128)S(1)}, f32[16,32,1024]{2,1,0:T(8,128)S(1)}) custom-call(s32[8,3]{1,0:T(8,128)S(1)} %copy.65.tiles_ref, f32[16,16,32,3]{3,2,1,0:T(8,128)S(1)} %bitcast.63, f32[8,1024]{1,0:T(8,128)S(1)} %stack.12.lanes_ref), custom_call_target="tpu_custom_call" | custom-call | flops 20971520 | bytes 4194304 | tf_op jit(solution)/shard_map/pallas_call | solution.py:64
  42.8 1.3 copy-done
  44.1 1.3 copy-done.5
  45.6 8.2 %all-gather.6.cloned.1.call-done = f32[512,1024]{1,0:T(8,128)} async-done(((f32[32,1024]{1,0:T(8,128)}), f32[512,1024]{1,0:T(8,128)}) %all-gather.6.cloned.1.call-update) | async-done | bytes 2097168 | tf_op jit(solution)/shard_map/all_gather | solution.py:215
  53.8 1.6 copy-done.1
  55.3 1.6 copy-done.6
  56.9 1.6 copy-done.12
  58.5 10.7 %shard_map.74 = f32[16,32,1024]{2,1,0:T(8,128)S(1)} custom-call(s32[8,3]{1,0:T(8,128)S(1)} %copy.65.tiles_ref, f32[16,32,1024]{2,1,0:T(8,128)S(1)} %bitcast.66, f32[16,32,1024]{2,1,0:T(8,128)S(1)} %bitcast.67, f32[16,32,1024]{2,1,0:T(8,128)S(1)} %copy-done.1, f32[16,32,1024]{2,1,0:T(8,128)S(1)} %copy-done.6, bf16[8,1024,64]{2,1,0:T(8,128)(2,1)S(1)} %copy.66.vis_ref, ...), custom_call_target="tpu_custom_call" | custom-call | flops 2415919104 | bytes 6029312 | tf_op jit(solution)/shard_map/pallas_call | solution.py:176
  69.2 1.4 copy-done.17
  71.3 24.8 %all-gather.10.cloned.1.call-done = f32[512,1024]{1,0:T(8,128)} async-done(((f32[32,1024]{1,0:T(8,128)}), f32[512,1024]{1,0:T(8,128)}) %all-gather.10.cloned.1.call-update) | async-done | bytes 2097168 | tf_op jit(solution)/shard_map/all_gather | solution.py:215
  96.1 1.6 copy-done.2
  97.7 1.6 copy-done.7
  99.3 1.6 copy-done.11
  100.9 10.7 %shard_map.76 = f32[16,32,1024]{2,1,0:T(8,128)S(1)} custom-call(s32[8,3]{1,0:T(8,128)S(1)} %copy.65.tiles_ref, f32[16,32,1024]{2,1,0:T(8,128)S(1)} %bitcast.64, f32[16,32,1024]{2,1,0:T(8,128)S(1)} %bitcast.65, f32[16,32,1024]{2,1,0:T(8,128)S(1)} %copy-done.2, f32[16,32,1024]{2,1,0:T(8,128)S(1)} %copy-done.7, bf16[8,1024,64]{2,1,0:T(8,128)(2,1)S(1)} %copy.66.vis_ref, ...), custom_call_target="tpu_custom_call" | custom-call | flops 2415919104 | bytes 6029312 | tf_op jit(solution)/shard_map/pallas_call | solution.py:176
  111.6 1.4 copy-done.16
  113.7 19.3 %all-gather = s32[16,8,3]{1,2,0:T(4,128)S(1)} all-gather(s32[1,8,3]{1,2,0:T(4,128)S(1)} %bitcast.79), channel_id=1, replica_groups=mesh['group'=2,'tile'=16] {'tile'}, dimensions={0}, use_global_device_ids=true | all-gather | bytes 1632 | tf_op jit(solution)/shard_map/all_gather | solution.py:215
  133.2 19.9 %all_gather.20 = f32[128,1024]{1,0:T(8,128)S(1)} all-gather(f32[8,1024]{1,0:T(8,128)S(1)} %select_convert_fusion), channel_id=1, replica_groups=mesh['group'=2,'tile'=16] {'tile'}, dimensions={0}, use_global_device_ids=true | all-gather | bytes 557056 | tf_op jit(solution)/shard_map/all_gather | solution.py:215
  154.5 2.4 fusion.7
  156.9 4.4 reduce-scatter.5.cloned.1.call-done
  161.3 1.6 fusion.16
  163.1 2.4 fusion.3
  165.4 60.6 %reduce-scatter.9.cloned.1.call-done = f32[32,1024]{1,0:T(8,128)} async-done(((f32[512,1024]{1,0:T(8,128)}), f32[32,1024]{1,0:T(8,128)}) %reduce-scatter.9.cloned.1.call-update) | async-done | bytes 131088 | tf_op jit(solution)/shard_map/reduce_scatter | solution.py:275
  226.0 1.6 fusion.18
  227.8 40.6 %all-gather.8.cloned.1.call-done = f32[512,1024]{1,0:T(8,128)} async-done(((f32[32,1024]{1,0:T(8,128)}), f32[512,1024]{1,0:T(8,128)}) %all-gather.8.cloned.1.call-update) | async-done | bytes 2097168 | tf_op jit(solution)/shard_map/all_gather | solution.py:215
  268.5 1.6 copy-done.3
  270.0 1.6 copy-done.8
  271.6 1.6 copy-done.13
  273.2 10.7 %shard_map.75 = f32[16,32,1024]{2,1,0:T(8,128)S(1)} custom-call(s32[8,3]{1,0:T(8,128)S(1)} %copy.65.tiles_ref, f32[16,32,1024]{2,1,0:T(8,128)S(1)} %bitcast.68, f32[16,32,1024]{2,1,0:T(8,128)S(1)} %bitcast.69, f32[16,32,1024]{2,1,0:T(8,128)S(1)} %copy-done.3, f32[16,32,1024]{2,1,0:T(8,128)S(1)} %copy-done.8, bf16[8,1024,64]{2,1,0:T(8,128)(2,1)S(1)} %copy.66.vis_ref, ...), custom_call_target="tpu_custom_call" | custom-call | flops 2415919104 | bytes 6029312 | tf_op jit(solution)/shard_map/pallas_call | solution.py:176
  283.9 1.4 copy-done.18
  285.4 25.3 %all-gather.12.cloned.1.call-done = f32[512,1024]{1,0:T(8,128)} async-done(((f32[32,1024]{1,0:T(8,128)}), f32[512,1024]{1,0:T(8,128)}) %all-gather.12.cloned.1.call-update) | async-done | bytes 2097168 | tf_op jit(solution)/shard_map/all_gather | solution.py:215
  310.7 1.6 copy-done.4
  312.3 1.6 copy-done.9
  313.9 1.6 copy-done.15
  315.4 10.7 %shard_map.77 = f32[16,32,1024]{2,1,0:T(8,128)S(1)} custom-call(s32[8,3]{1,0:T(8,128)S(1)} %copy.65.tiles_ref, f32[16,32,1024]{2,1,0:T(8,128)S(1)} %bitcast.70, f32[16,32,1024]{2,1,0:T(8,128)S(1)} %bitcast.71, f32[16,32,1024]{2,1,0:T(8,128)S(1)} %copy-done.4, f32[16,32,1024]{2,1,0:T(8,128)S(1)} %copy-done.9, bf16[8,1024,64]{2,1,0:T(8,128)(2,1)S(1)} %copy.66.vis_ref, ...), custom_call_target="tpu_custom_call" | custom-call | flops 2415919104 | bytes 6029312 | tf_op jit(solution)/shard_map/pallas_call | solution.py:176
  326.1 1.3 copy-done.19
  327.5 2.6 fusion.1
  330.9 43.9 %reduce-scatter.7.cloned.1.call-done = f32[32,1024]{1,0:T(8,128)} async-done(((f32[512,1024]{1,0:T(8,128)}), f32[32,1024]{1,0:T(8,128)}) %reduce-scatter.7.cloned.1.call-update) | async-done | bytes 131088 | tf_op jit(solution)/shard_map/reduce_scatter | solution.py:275
  374.8 0.9 fusion.17
  375.9 63.8 %reduce-scatter.11.cloned.1.call-done = f32[32,1024]{1,0:T(8,128)} async-done(((f32[512,1024]{1,0:T(8,128)}), f32[32,1024]{1,0:T(8,128)}) %reduce-scatter.11.cloned.1.call-update) | async-done | bytes 131088 | tf_op jit(solution)/shard_map/reduce_scatter | solution.py:275
  439.7 0.9 fusion.19
  441.5 1.2 reshape.108
  (107 shorter events, 9.7 us)
Async XLA Ops:
  6.5 47.2 %all-gather.6.cloned.1.call-start = ((), (), s32[]{:S(2)}) async-start(), calls=%async_computation.4 | async-start | bytes 2228224 | tf_op jit(solution)/shard_map/all_gather | solution.py:215
  8.5 2.1 copy-start.30
  8.5 2.2 copy-start.32
  8.5 2.7 copy-start.29
  8.5 3.4 copy-start.26
  8.5 3.6 copy-start.24
  9.5 86.6 %all-gather.10.cloned.1.call-start = ((), (), s32[]{:S(2)}) async-start(), calls=%async_computation.8 | async-start | bytes 2228224 | tf_op jit(solution)/shard_map/all_gather | solution.py:215
  10.5 150.9 %reduce-scatter.5.cloned.1.call-start = ((), (), s32[]{:S(2)}) async-start(), calls=%async_computation.5 | async-start | bytes 2228224 | tf_op jit(solution)/shard_map/reduce_scatter | solution.py:275
  31.6 1.1 copy-start.25
  35.4 2.4 copy-start.10
  42.8 1.3 copy-start
  44.1 1.3 copy-start.5
  53.8 1.6 copy-start.1
  55.3 1.6 copy-start.6
  56.9 1.6 copy-start.12
  69.2 1.4 copy-start.17
  70.6 0.7 copy-start.28
  70.6 155.4 %reduce-scatter.9.cloned.1.call-start = ((), (), s32[]{:S(2)}) async-start(), calls=%async_computation.9 | async-start | bytes 2228224 | tf_op jit(solution)/shard_map/reduce_scatter | solution.py:275
  96.1 1.6 copy-start.2
  97.7 1.6 copy-start.7
  99.3 1.6 copy-start.11
  111.6 1.4 copy-start.16
  113.0 0.7 copy-start.27
  113.0 0.8 copy-start.31
  113.0 155.5 %all-gather.8.cloned.1.call-start = ((), (), s32[]{:S(2)}) async-start(), calls=%async_computation.6 | async-start | bytes 2228224 | tf_op jit(solution)/shard_map/all_gather | solution.py:215
  153.6 7.8 %copy-start.21 = (f32[32,1024]{1,0:T(8,128)S(1)}, f32[32,1024]{1,0:T(8,128)}, u32[]{:S(2)}) copy-start(f32[32,1024]{1,0:T(8,128)} %reshape_squeeze.6) | copy-start | bytes 393220
  154.4 71.6 %copy-start.20 = (f32[32,1024]{1,0:T(8,128)S(1)}, f32[32,1024]{1,0:T(8,128)}, u32[]{:S(2)}) copy-start(f32[32,1024]{1,0:T(8,128)} %reshape_squeeze.7) | copy-start | bytes 393220
  162.9 147.7 %all-gather.12.cloned.1.call-start = ((), (), s32[]{:S(2)}) async-start(), calls=%async_computation.10 | async-start | bytes 2228224 | tf_op jit(solution)/shard_map/all_gather | solution.py:215
  227.6 147.2 %reduce-scatter.7.cloned.1.call-start = ((), (), s32[]{:S(2)}) async-start(), calls=%async_computation.7 | async-start | bytes 2228224 | tf_op jit(solution)/shard_map/reduce_scatter | solution.py:275
  268.4 1.6 copy-start.3
  270.0 1.6 copy-start.8
  271.6 1.6 copy-start.13
  283.9 1.4 copy-start.18
  285.3 154.4 %reduce-scatter.11.cloned.1.call-start = ((), (), s32[]{:S(2)}) async-start(), calls=%async_computation.11 | async-start | bytes 2228224 | tf_op jit(solution)/shard_map/reduce_scatter | solution.py:275
  310.7 1.6 copy-start.4
  312.3 1.6 copy-start.9
  313.9 1.6 copy-start.15
  326.1 1.3 copy-start.19
  327.5 2.6 copy-start.14
  327.5 47.4 %copy-start.22 = (f32[32,1024]{1,0:T(8,128)S(1)}, f32[32,1024]{1,0:T(8,128)}, u32[]{:S(2)}) copy-start(f32[32,1024]{1,0:T(8,128)} %fusion.16) | copy-start | bytes 393220
  327.5 112.2 %copy-start.23 = (f32[32,1024]{1,0:T(8,128)S(1)}, f32[32,1024]{1,0:T(8,128)}, u32[]{:S(2)}) copy-start(f32[32,1024]{1,0:T(8,128)} %fusion.18) | copy-start | bytes 393220
Sparse Core Ops, SparseCore 0:
  9.6 44.0 all-gather.5
  55.9 40.1 all-gather.9
  99.9 61.4 reduce-scatter.4
  165.4 60.5 reduce-scatter.8
  228.0 40.4 all-gather.7
  270.5 40.1 all-gather.11
  314.4 60.3 reduce-scatter.6
  379.0 60.6 reduce-scatter.10

commit v2 on v1

--- a/solution.py
+++ b/solution.py
@@ -10,7 +10,7 @@
 
 SB = 32
 ITERS = 2
-GROUPS = 2
+GROUPS = 1
 LANES = 128
 VMEM = 40 * 1024 * 1024
 
@@ -199,7 +199,287 @@
     )(tiles, gathered, gathered, cosine, sine_part, vis_rows, weights, flux_row)
 
 
-def on_device(gains, tiles, vis, flags, station_uvw, src_lm, flux):
+class Line:
+    def __init__(self, count):
+        chips = count // 2
+        self.cols = 1
+        while (2 * self.cols) ** 2 <= chips:
+            self.cols *= 2
+        self.rows = chips // self.cols
+        me = lax.axis_index("tile")
+        self.me = me
+        self.c = lax.rem(me, 2)
+        self.b = lax.rem(me // 2, self.cols)
+        self.a = me // (2 * self.cols)
+
+    def index(self, a, b, c):
+        return (a * self.cols + b) * 2 + c
+
+    def has_row(self, a):
+        return (a >= 0) & (a < self.rows)
+
+    def has_col(self, b):
+        return (b >= 0) & (b < self.cols)
+
+    def greet(self):
+        barrier = pltpu.get_barrier_semaphore()
+        near = [(self.a + d, self.b, self.has_row(self.a + d)) for d in (1, -1)]
+        near += [(self.a, self.b + d, self.has_col(self.b + d)) for d in (1, -1)]
+        total = 1
+        pl.semaphore_signal(
+            barrier, inc=1, device_id={"tile": self.index(self.a, self.b, 1 - self.c)}
+        )
+        for a, b, there in near:
+            total = total + there.astype(jnp.int32)
+
+            @pl.when(there)
+            def _():
+                pl.semaphore_signal(
+                    barrier, inc=1, device_id={"tile": self.index(a, b, self.c)}
+                )
+
+        pl.semaphore_wait(barrier, total)
+
+
+def signed(distance):
+    return [(distance, 1), (distance, -1)] if distance else [(0, 0)]
+
+
+UP, DOWN, RIGHT, LEFT, CORE = range(5)
+
+
+def gather_kernel(count, arrays, *refs):
+    ins, outs = refs[:arrays], refs[arrays : 2 * arrays]
+    send, recv = refs[2 * arrays :]
+    at = Line(count)
+    for n in range(arrays):
+        outs[n][at.me] = ins[n][...]
+    at.greet()
+
+    def copies(origin, target, way):
+        return [
+            pltpu.make_async_remote_copy(
+                src_ref=outs[n].at[origin],
+                dst_ref=outs[n].at[origin],
+                send_sem=send.at[n, way, origin],
+                recv_sem=recv.at[n, origin],
+                device_id={"tile": target},
+            )
+            for n in range(arrays)
+        ]
+
+    partner = at.index(at.a, at.b, 1 - at.c)
+
+    def visit(finish):
+        def emit(origin, target, way):
+            for copy in copies(origin, target, way):
+                if finish:
+                    copy.wait_send()
+                else:
+                    copy.start()
+
+        for clock in range(at.rows + at.cols - 1):
+            for s in range(max(0, clock - at.cols + 1), min(clock, at.rows - 1) + 1):
+                for s_, va in signed(s):
+                    for t_, vb in signed(clock - s):
+                        a, b = at.a - s_ * va, at.b - t_ * vb
+
+                        @pl.when(at.has_row(a) & at.has_col(b))
+                        def _():
+                            origin = at.index(a, b, at.c)
+                            if clock and not finish:
+                                for copy in copies(origin, partner, CORE):
+                                    copy.wait_recv()
+                            if t_ == 0:
+                                for way, step in ((UP, 1), (DOWN, -1)):
+                                    if va in (0, step):
+
+                                        @pl.when(at.has_row(at.a + step))
+                                        def _():
+                                            emit(origin, at.index(at.a + step, at.b, at.c), way)
+
+                            for way, step in ((RIGHT, 1), (LEFT, -1)):
+                                if vb in (0, step):
+
+                                    @pl.when(at.has_col(at.b + step))
+                                    def _():
+                                        emit(origin, at.index(at.a, at.b + step, at.c), way)
+
+                            emit(origin, partner, CORE)
+
+    visit(False)
+    for chip in range(at.rows * at.cols):
+        for copy in copies(2 * chip + 1 - at.c, partner, CORE):
+            copy.wait_recv()
+    visit(True)
+
+
+def gather_all(count, call, *arrays):
+    number = len(arrays)
+    return pl.pallas_call(
+        functools.partial(gather_kernel, count, number),
+        out_shape=[jax.ShapeDtypeStruct((count,) + x.shape, x.dtype) for x in arrays],
+        in_specs=[pl.BlockSpec(memory_space=pltpu.VMEM)] * number,
+        out_specs=[pl.BlockSpec(memory_space=pltpu.VMEM)] * number,
+        scratch_shapes=[
+            pltpu.SemaphoreType.DMA((number, 5, count)),
+            pltpu.SemaphoreType.DMA((number, count)),
+        ],
+        compiler_params=pltpu.CompilerParams(
+            collective_id=call, has_side_effects=True, vmem_limit_bytes=VMEM
+        ),
+    )(*arrays)
+
+
+def scatter_kernel(
+    count, x, out, from_core, from_col, to_col, from_row, to_row,
+    core_send, core_recv, col_send, col_recv, row_send, row_recv
+):
+    at = Line(count)
+    at.greet()
+    partner = at.index(at.a, at.b, 1 - at.c)
+
+    def core_copy(chip):
+        return pltpu.make_async_remote_copy(
+            src_ref=x.at[2 * chip + 1 - at.c],
+            dst_ref=from_core.at[chip],
+            send_sem=core_send.at[chip],
+            recv_sem=core_recv.at[chip],
+            device_id={"tile": partner},
+        )
+
+    def col_copy(chip, way, step):
+        return pltpu.make_async_remote_copy(
+            src_ref=to_col.at[chip],
+            dst_ref=from_col.at[way, chip],
+            send_sem=col_send.at[chip],
+            recv_sem=col_recv.at[way, chip],
+            device_id={"tile": at.index(at.a, at.b + step, at.c)},
+        )
+
+    def row_copy(a, way, step):
+        return pltpu.make_async_remote_copy(
+            src_ref=to_row.at[a],
+            dst_ref=from_row.at[way, a],
+            send_sem=row_send.at[a],
+            recv_sem=row_recv.at[way, a],
+            device_id={"tile": at.index(at.a + step, at.b, at.c)},
+        )
+
+    def each_row(body):
+        for s in reversed(range(at.rows)):
+            for s_, va in signed(s):
+                a = at.a + s_ * va
+
+                @pl.when(at.has_row(a))
+                def _():
+                    body(a, va)
+
+    def each_far_col(body):
+        for t in reversed(range(1, at.cols)):
+            for t_, vb in signed(t):
+                b = at.b + t_ * vb
+
+                @pl.when(at.has_col(b))
+                def _():
+                    body(b, vb)
+
+    def start_core(a, va):
+        each_far_col(lambda b, vb: core_copy(a * at.cols + b).start())
+
+    def start_core_near(a, va):
+        core_copy(a * at.cols + at.b).start()
+
+    each_row(start_core)
+    each_row(start_core_near)
+
+    def pass_col(a, va):
+        def far(b, vb):
+            chip = a * at.cols + b
+            core_copy(chip).wait_recv()
+            to_col[chip] = x[2 * chip + at.c] + from_core[chip]
+            way = 0 if vb > 0 else 1
+
+            @pl.when(at.has_col(at.b - vb))
+            def _():
+                col_copy(chip, way, vb).wait_recv()
+                to_col[chip] += from_col[way, chip]
+
+            col_copy(chip, way, vb).start()
+
+        each_far_col(far)
+
+    each_row(pass_col)
+
+    def pass_row(a, va):
+        chip = a * at.cols + at.b
+        core_copy(chip).wait_recv()
+        to_row[a] = x[2 * chip + at.c] + from_core[chip]
+        for way, step in ((0, 1), (1, -1)):
+
+            @pl.when(at.has_col(at.b - step))
+            def _():
+                col_copy(chip, way, step).wait_recv()
+                to_row[a] += from_col[way, chip]
+
+        for way, step in ((0, 1), (1, -1)):
+            if va in (0, step):
+
+                @pl.when(at.has_row(at.a - step))
+                def _():
+                    row_copy(a, way, step).wait_recv()
+                    to_row[a] += from_row[way, a]
+
+        if va == 0:
+            out[...] = to_row[a]
+        else:
+            row_copy(a, 0 if va > 0 else 1, va).start()
+
+    each_row(pass_row)
+
+    def finish(a, va):
+        each_far_col(lambda b, vb: col_copy(a * at.cols + b, 0, vb).wait_send())
+        if va:
+            row_copy(a, 0, va).wait_send()
+
+    each_row(finish)
+    for chip in range(at.rows * at.cols):
+        core_copy(chip).wait_send()
+
+
+def scatter_sum(count, call, x):
+    piece = x.shape[1:]
+    chips = count // 2
+    cols = 1
+    while (2 * cols) ** 2 <= chips:
+        cols *= 2
+    rows = chips // cols
+    slots = lambda *lead: pltpu.VMEM(lead + piece, x.dtype)
+    return pl.pallas_call(
+        functools.partial(scatter_kernel, count),
+        out_shape=jax.ShapeDtypeStruct(piece, x.dtype),
+        in_specs=[pl.BlockSpec(memory_space=pltpu.VMEM)],
+        out_specs=pl.BlockSpec(memory_space=pltpu.VMEM),
+        scratch_shapes=[
+            slots(chips),
+            slots(2, chips),
+            slots(chips),
+            slots(2, rows),
+            slots(rows),
+            pltpu.SemaphoreType.DMA((chips,)),
+            pltpu.SemaphoreType.DMA((chips,)),
+            pltpu.SemaphoreType.DMA((chips,)),
+            pltpu.SemaphoreType.DMA((2, chips)),
+            pltpu.SemaphoreType.DMA((rows,)),
+            pltpu.SemaphoreType.DMA((2, rows)),
+        ],
+        compiler_params=pltpu.CompilerParams(
+            collective_id=call, has_side_effects=True, vmem_limit_bytes=VMEM
+        ),
+    )(x)
+
+
+def on_device(count, gains, tiles, vis, flags, station_uvw, src_lm, flux):
     dirs, chans = flux.shape
     times, _, stations = station_uvw.shape
     items = tiles.shape[0]
@@ -211,18 +491,19 @@
     turned = gains.reshape(owned_count, dirs, 2, GROUPS, per).transpose(3, 0, 2, 4, 1)
     owned = [turned[g].reshape(owned_count, 2 * width) for g in range(GROUPS)]
 
-    def gather(x):
-        return lax.all_gather(x, "tile", axis=0, tiled=True)
-
-    gathered = [gather(x) for x in owned]
-
     keep = jnp.logical_or(
         (tiles[:, 0] != tiles[:, 1])[:, None],
         (jnp.arange(SB)[:, None] > jnp.arange(SB)[None, :]).reshape(1, SB * SB),
     )
     weights = jnp.where(keep, flags, 0).astype(jnp.float32)
-    all_weights = gather(weights)
-    all_tiles = gather(tiles)
+    extra = jnp.pad(tiles.astype(jnp.float32), ((0, 0), (0, LANES - 3)))
+    full_gains, described = gather_all(
+        count, 0, owned[0], jnp.concatenate([weights, extra], axis=1)
+    )
+    gathered = [full_gains.reshape(stations, 2 * width)]
+    described = described.reshape(count * items, SB * SB + LANES)
+    all_weights = described[:, : SB * SB]
+    all_tiles = described[:, SB * SB : SB * SB + 3].astype(jnp.int32)
 
     source_l, source_m = src_lm[0], src_lm[1]
     squares = source_l * source_l + source_m * source_m
@@ -271,8 +552,8 @@
                 vis_rows,
                 pair_weights,
                 flux_rows[g],
-            ).reshape(stations, 2 * width)
-            share = lax.psum_scatter(numerator, "tile", scatter_dimension=0, tiled=True)
+            ).reshape(count, owned_count, 2 * width)
+            share = scatter_sum(count, 2, numerator)
             power = full[:, :width] * full[:, :width] + full[:, width:] * full[:, width:]
             denominator = (flux_rows[g] * flux_rows[g]) * jnp.dot(
                 pair_counts, power, precision=highest
@@ -281,7 +562,8 @@
             updated.append(owned[g] + share * jnp.concatenate([scale, scale], axis=1))
         owned = updated
         if iteration + 1 < ITERS:
-            gathered = [gather(x) for x in owned]
+            (full_gains,) = gather_all(count, 1, owned[0])
+            gathered = [full_gains.reshape(stations, 2 * width)]
 
     stacked = jnp.stack(owned).reshape(GROUPS, owned_count, 2, per, dirs)
     return stacked.transpose(1, 4, 2, 0, 3).reshape(owned_count * dirs, 2 * chans)
@@ -298,5 +580,5 @@
         P(),
     )
     return jax.shard_map(
-        on_device, mesh=mesh, in_specs=placed, out_specs=P(("group", "tile"), None), check_vma=False
-    )
+        functools.partial(on_device, mesh.shape["tile"]), mesh=mesh, in_specs=placed, out_specs=P(("group", "tile"), None), check_vma=False
+    )

time: 451 us -> 238 us (0.53)
  waiting for transfers between devices: 272 us -> 0 us
  Pallas kernels: 47.5 us -> 182 us
  blocking collectives: 39.2 us -> 0 us
  local copies, waits for them, and re-layouts: 61.8 us -> 44.9 us
  between operations: 13.9 us -> 0.26 us
    reduce_scatter x4 -> x0, waiting for transfers between devices: 173 us -> none  [on_device(): share = lax.psum_scatter(numerator, 'tile', scatter_dimension=0, tiled=True)]
    pallas_call x0 -> x4, Pallas kernels: none -> 135 us  [the longest x2 73.7 us: gather_all(): pl.pallas_call(functools.partial(gather_kernel, count, number), out_shape...]
    all_gather x4 -> x0, waiting for transfers between devices: 98.9 us -> none  [gather(): return lax.all_gather(x, 'tile', axis=0, tiled=True)]
    all_gather x2 -> x0, blocking collectives: 39.2 us -> none  [gather(): return lax.all_gather(x, 'tile', axis=0, tiled=True)]
    unnamed x70 -> x23, local copies, waits for them, and re-layouts: 33.8 us -> 13.8 us
    add x4 -> x2, other arithmetic: 5 us -> 0.09 us  [on_device(): updated.append(owned[g] + share * jnp.concatenate([scale, scale], axis=1))]
    pallas_call x4 -> x2, Pallas kernels: 42.7 us -> 42.8 us  [normal_terms(): pl.pallas_call(normal_kernel, grid_spec=pltpu.PrefetchScalarGridSpec(num_...]
  transfers between devices with their start and end apart: 8 -> 0, of which waited for: 8 -> 0; matrix products, arithmetic and copies ran while one was open for 9% -> 0% of each run, Pallas kernels for 11% -> 0%
where the time goes in v2:
time: 238 us; the launch traced here: 237 us
  Pallas kernels  182 us (76%)
  local copies, waits for them, and re-layouts  44.9 us (19%)
  matrix products  6.08 us (3%)
  other arithmetic  3.5 us (1%)
    pallas_call x2, Pallas kernels, gather_all(): pl.pallas_call(functools.partial(gather_kernel, count, number), out_shape...  73.7 us
    pallas_call x2, Pallas kernels, scatter_sum(): pl.pallas_call(functools.partial(scatter_kernel, count), out_shape=jax.Sh...  61.1 us
    pallas_call x2, Pallas kernels, normal_terms(): pl.pallas_call(normal_kernel, grid_spec=pltpu.PrefetchScalarGridSpec(num_...  42.8 us
    reshape x2, local copies, waits for them, and re-layouts, on_device(): vis_rows = vis.reshape(items, 2, chans, SB, SB).transpose(0, 2, 3, 1, 4)  15.3 us
    unnamed x23, local copies, waits for them, and re-layouts  13.8 us
    reshape x2, local copies, waits for them, and re-layouts, on_device(): vis_rows = vis_rows.reshape(items, chans * SB, 2 * SB)  9.12 us
    dot_general x2, matrix products, on_device(): jnp.dot(pair_counts, power, precision=highest)  5.38 us
    pallas_call x1, Pallas kernels, phasors(): pl.pallas_call(phasor_kernel, grid_spec=pltpu.PrefetchScalarGridSpec(num_...  4.88 us

profile of v2, /device:TPU:0, one launch (start us, length us, event | category | flops | bytes accessed | tf_op | source)
XLA Modules:
  0.0 237.2 jit_solution(14617167407095060289)
XLA Ops:
  0.0 0.8 compare_bitcast_fusion.2
  0.8 0.8 fusion.38
  1.5 0.8 copy.25.tiles_ref
  2.3 0.1 gt.23
  2.4 0.1 stack_tile.11
  2.6 0.1 stack_reshape.15
  2.6 0.1 stack_tile.10
  2.7 0.1 stack_tile.9
  2.9 0.8 copy.24
  3.7 0.1 squeeze_reshape.2.flux_ref
  3.8 0.7 bitcast_multiply_fusion
  4.6 0.1 mul.58
  4.6 0.8 select_convert_fusion
  5.5 0.1 reshape.63
  5.6 0.1 pad_maximum_fusion.w_ref
  5.7 1.3 reshape.59
  7.0 0.6 copy.37
  7.6 0.5 reshape_squeeze.3.refs_0_
  8.1 6.3 %reshape.61 = bf16[8,2,32,32,32]{4,3,2,1,0:T(8,128)(2,1)} reshape(bf16[8,2,32,1024]{3,2,1,0:T(8,128)(2,1)} %param.9) | data formatting | bytes 2097152 | tf_op jit(solution)/shard_map/reshape | solution.py:519
  14.4 9.0 %copy.23 = bf16[8,2,32,32,32]{3,2,4,1,0:T(8,128)(2,1)} copy(bf16[8,2,32,32,32]{4,3,2,1,0:T(8,128)(2,1)} %reshape.61) | data formatting | bytes 2097152 | tf_op jit(solution)/shard_map/reshape | solution.py:519
  23.3 7.0 %reshape.62 = bf16[8,1024,64]{1,2,0:T(8,128)(2,1)} reshape(bf16[8,32,32,2,32]{2,1,4,3,0:T(8,128)(2,1)} %bitcast.55) | data formatting | bytes 2097152 | tf_op jit(solution)/shard_map/reshape | solution.py:520
  30.3 2.1 copy.26.vis_ref
  32.5 2.6 %copy.21 = f32[16,3,512]{1,2,0:T(8,128)} copy(f32[16,3,512]{2,0,1:T(8,128)S(1)} %copy-done.9) | data formatting | bytes 196608 | tf_op args[4]
  35.1 2.2 copy-done.2
  37.3 4.9 %shard_map.74 = (f32[16,32,1024]{2,1,0:T(8,128)S(1)}, f32[16,32,1024]{2,1,0:T(8,128)S(1)}) custom-call(s32[8,3]{1,0:T(8,128)S(1)} %copy.25.tiles_ref, f32[16,16,32,3]{3,2,1,0:T(8,128)S(1)} %bitcast.50, f32[8,1024]{1,0:T(8,128)S(1)} %stack.3.lanes_ref), custom_call_target="tpu_custom_call" | custom-call | flops 20971520 | bytes 4194304 | tf_op jit(solution)/shard_map/pallas_call | solution.py:64
  42.2 1.3 copy-done.4
  43.5 1.3 copy-done.6
  44.9 40.9 %shard_map.73 = (f32[16,32,2048]{2,1,0:T(8,128)S(1)}, f32[16,8,1152]{2,1,0:T(8,128)S(1)}) custom-call(f32[32,2048]{1,0:T(8,128)S(1)} %reshape_squeeze.3.refs_0_, f32[8,1152]{1,0:T(8,128)S(1)} %select_maximum_fusion.refs_1_), custom_call_target="tpu_custom_call" | custom-call | tf_op jit(solution)/shard_map/pallas_call | solution.py:319
  85.8 1.9 copy-done.3
  87.9 0.3 fusion.26
  88.2 0.3 fusion.24
  88.6 0.1 reshape.66
  88.7 0.2 copy.30
  88.9 0.1 reshape.65
  89.0 0.2 bitcast_add_fusion
  89.1 0.1 reshape.67
  89.3 3.9 %fusion.12 = f32[32,1024]{1,0:T(8,128)S(1)} fusion(f32[32,512]{1,0:T(8,128)S(1)} %reshape.67, f32[512,2048]{1,0:T(8,128)} %bitcast.51, f32[1024]{0:T(1024)S(1)} %mul.58), kind=kOutput, calls=%fused_computation.10 | convolution fusion | flops 202997760 | bytes 4395008 | tf_op jit(solution)/shard_map/dot_general | solution.py:558
  93.2 1.6 copy-done.7
  94.8 21.4 %shard_map.75.x = f32[16,32,2048]{2,1,0:T(8,128)S(1)} custom-call(s32[8,3]{1,0:T(8,128)S(1)} %copy.25.tiles_ref, f32[16,32,2048]{2,1,0:T(8,128)} %copy-done.3, f32[16,32,2048]{2,1,0:T(8,128)} %copy-done.3, f32[16,32,1024]{2,1,0:T(8,128)S(1)} %copy-done.5, f32[16,32,1024]{2,1,0:T(8,128)S(1)} %copy-done.7, bf16[8,1024,64]{2,1,0:T(8,128)(2,1)S(1)} %copy.26.vis_ref, ...), custom_call_target="tpu_custom_call" | custom-call | flops 4831838208 | bytes 12058624 | tf_op jit(solution)/shard_map/pallas_call | solution.py:176
  116.2 30.0 %shard_map.76 = f32[32,2048]{1,0:T(8,128)S(1)} custom-call(f32[16,32,2048]{2,1,0:T(8,128)S(1)} %shard_map.75.x), custom_call_target="tpu_custom_call" | custom-call | tf_op jit(solution)/shard_map/pallas_call | solution.py:458
  146.3 32.8 %shard_map.77.grow_ref.gcol_ref = f32[16,32,2048]{2,1,0:T(8,128)S(1)} custom-call(f32[32,2048]{1,0:T(8,128)S(1)} %fusion.28.refs_0_), custom_call_target="tpu_custom_call" | custom-call | tf_op jit(solution)/shard_map/pallas_call | solution.py:319
  179.1 1.9 copy-done
  181.0 21.4 %shard_map.78.x = f32[16,32,2048]{2,1,0:T(8,128)S(1)} custom-call(s32[8,3]{1,0:T(8,128)S(1)} %copy.25.tiles_ref, f32[16,32,2048]{2,1,0:T(8,128)} %copy-done, f32[16,32,2048]{2,1,0:T(8,128)} %copy-done, f32[16,32,1024]{2,1,0:T(8,128)S(1)} %copy-done.5, f32[16,32,1024]{2,1,0:T(8,128)S(1)} %copy-done.8, bf16[8,1024,64]{2,1,0:T(8,128)(2,1)S(1)} %copy.26.vis_ref, ...), custom_call_target="tpu_custom_call" | custom-call | flops 4831838208 | bytes 12058624 | tf_op jit(solution)/shard_map/pallas_call | solution.py:176
  202.4 31.0 %shard_map.79 = f32[32,2048]{1,0:T(8,128)S(1)} custom-call(f32[16,32,2048]{2,1,0:T(8,128)S(1)} %shard_map.78.x), custom_call_target="tpu_custom_call" | custom-call | tf_op jit(solution)/shard_map/pallas_call | solution.py:458
  233.4 1.5 fusion.21
  235.0 0.3 reshape_stack.3
  235.3 0.6 copy.33
  236.0 1.2 reshape.70
  (31 shorter events, 0.5 us)
Async XLA Ops:
  30.3 2.1 copy-start.9
  35.1 2.2 copy-start.2
  42.2 1.3 copy-start.4
  43.5 1.3 copy-start.6
  85.8 1.9 copy-start.3
  89.3 3.9 %copy-start.5 = (f32[16,32,1024]{2,1,0:T(8,128)S(1)}, f32[16,32,1024]{2,1,0:T(8,128)}, u32[]{:S(2)}) copy-start(f32[16,32,1024]{2,1,0:T(8,128)} %copy-done.4) | copy-start | bytes 6291460
  93.2 1.6 copy-start.7
  146.3 34.7 %copy-start.8 = (f32[16,32,1024]{2,1,0:T(8,128)S(1)}, f32[16,32,1024]{2,1,0:T(8,128)}, u32[]{:S(2)}) copy-start(f32[16,32,1024]{2,1,0:T(8,128)} %copy-done.6) | copy-start | bytes 6291460
  179.0 1.9 copy-start
  202.4 31.0 %copy-start.1 = (f32[16,32,2048]{2,1,0:T(8,128)S(1)}, f32[16,32,2048]{2,1,0:T(8,128)}, u32[]{:S(2)}) copy-start(f32[16,32,2048]{2,1,0:T(8,128)} %copy-done) | copy-start | bytes 12582916

commit v3 on v2

--- a/solution.py
+++ b/solution.py
@@ -150,7 +150,11 @@
             for j in range(2)
         ]
         model = dot(rows, cols, 1, 1)
-        observed = vis_ref[0, start : start + LANES, :].astype(jnp.float32)
+        seen = slice(start, start + LANES)
+        observed = jnp.concatenate(
+            [vis_ref[0, 0, seen, :].astype(jnp.float32), vis_ref[0, 1, seen, :].astype(jnp.float32)],
+            axis=1,
+        )
         resid = split((observed - model) * weights)
         srow = dot(resid, cols, 1, 0)
         cross = dot(resid, rows, 0, 0)
@@ -183,7 +187,7 @@
                 gain_spec(1),
                 turn_spec,
                 turn_spec,
-                pl.BlockSpec((1, width, 2 * SB), lambda i, t: (i, group, 0)),
+                pl.BlockSpec((1, 2, width, SB), lambda i, t: (i, 0, group, 0)),
                 pl.BlockSpec((1, SB, 2 * SB), lambda i, t: (i, 0, 0)),
                 pl.BlockSpec((1, width), lambda i, t: (0, 0)),
             ],
@@ -516,8 +520,7 @@
     uvw_columns = station_uvw.reshape(times, 3, blocks, SB).transpose(0, 2, 3, 1)
     cosine, sine_part = phasors(tiles, uvw_columns, lane_rows)
 
-    vis_rows = vis.reshape(items, 2, chans, SB, SB).transpose(0, 2, 3, 1, 4)
-    vis_rows = vis_rows.reshape(items, chans * SB, 2 * SB)
+    vis_rows = vis.reshape(items, 2, chans * SB, SB)
     square = weights.reshape(items, SB, SB)
     pair_weights = jnp.concatenate([square, square], axis=2)
     flux_rows = flux.T.reshape(GROUPS, 1, width)

time: 238 us -> 217 us (0.912)
  local copies, waits for them, and re-layouts: 44.9 us -> 24.2 us
    reshape x4 -> x1, local copies, waits for them, and re-layouts: 24.4 us -> 6.27 us  [on_device(): vis_rows = vis.reshape(items, 2, chans * SB, SB)]
    unnamed x23 -> x15, local copies, waits for them, and re-layouts: 13.8 us -> 11.2 us
where the time goes in v3:
time: 217 us; the launch traced here: 216 us
  Pallas kernels  182 us (84%)
  local copies, waits for them, and re-layouts  24.2 us (11%)
  matrix products  6.07 us (3%)
  other arithmetic  3.5 us (2%)
    pallas_call x2, Pallas kernels, gather_all(): pl.pallas_call(functools.partial(gather_kernel, count, number), out_shape...  73.7 us
    pallas_call x2, Pallas kernels, scatter_sum(): pl.pallas_call(functools.partial(scatter_kernel, count), out_shape=jax.Sh...  61.4 us
    pallas_call x2, Pallas kernels, normal_terms(): pl.pallas_call(normal_kernel, grid_spec=pltpu.PrefetchScalarGridSpec(num_...  42.4 us
    unnamed x15, local copies, waits for them, and re-layouts  11.2 us
    reshape x1, local copies, waits for them, and re-layouts, on_device(): vis_rows = vis.reshape(items, 2, chans * SB, SB)  6.27 us
    dot_general x2, matrix products, on_device(): jnp.dot(pair_counts, power, precision=highest)  5.38 us
    pallas_call x1, Pallas kernels, phasors(): pl.pallas_call(phasor_kernel, grid_spec=pltpu.PrefetchScalarGridSpec(num_...  4.88 us

profile of v3, /device:TPU:0, one launch (start us, length us, event | category | flops | bytes accessed | tf_op | source)
XLA Modules:
  0.0 216.4 jit_solution(6498855645963823133)
XLA Ops:
  0.0 0.8 compare_bitcast_fusion.2
  0.8 0.8 fusion.38
  1.5 0.8 copy.23.tiles_ref
  2.3 0.1 gt.23
  2.4 0.1 stack_tile.11
  2.5 0.1 broadcast_in_dim.20
  2.6 0.1 stack_reshape.15
  2.6 0.1 stack_tile.10
  2.7 0.1 stack_tile.9
  2.8 0.1 stack.3.lanes_ref
  2.9 0.8 copy.22
  3.7 0.1 squeeze_reshape.2.flux_ref
  3.8 0.7 bitcast_multiply_fusion
  4.5 0.1 copy.24
  4.6 0.1 mul.58
  4.6 0.8 select_convert_fusion
  5.5 0.1 reshape.59
  5.6 0.1 pad_maximum_fusion.w_ref
  5.7 1.3 reshape.56
  7.0 0.6 copy.33
  7.6 0.5 reshape_squeeze.3.refs_0_
  8.1 6.3 %reshape.58.vis_ref = bf16[8,2,1024,32]{3,2,1,0:T(8,128)(2,1)} reshape(bf16[8,2,32,1024]{3,2,1,0:T(8,128)(2,1)} %param.9) | data formatting | bytes 2097152 | tf_op jit(solution)/shard_map/reshape | solution.py:523
  14.4 2.6 %copy.20 = f32[16,3,512]{1,2,0:T(8,128)} copy(f32[16,3,512]{2,0,1:T(8,128)S(1)} %copy-done.5) | data formatting | bytes 196608 | tf_op args[4]
  17.0 2.2 %copy-done.2 = f32[16,3,512]{1,2,0:T(8,128)S(1)} copy-done((f32[16,3,512]{1,2,0:T(8,128)S(1)}, f32[16,3,512]{1,2,0:T(8,128)}, u32[]{:S(2)}) %copy-start.2) | copy-done | bytes 98328
  19.2 4.9 %shard_map.74 = (f32[16,32,1024]{2,1,0:T(8,128)S(1)}, f32[16,32,1024]{2,1,0:T(8,128)S(1)}) custom-call(s32[8,3]{1,0:T(8,128)S(1)} %copy.23.tiles_ref, f32[16,16,32,3]{3,2,1,0:T(8,128)S(1)} %bitcast.46, f32[8,1024]{1,0:T(8,128)S(1)} %stack.3.lanes_ref), custom_call_target="tpu_custom_call" | custom-call | flops 20971520 | bytes 4194304 | tf_op jit(solution)/shard_map/pallas_call | solution.py:64
  24.1 0.0 copy-start.3
  24.1 1.3 copy-done.3
  25.5 40.9 %shard_map.73 = (f32[16,32,2048]{2,1,0:T(8,128)S(1)}, f32[16,8,1152]{2,1,0:T(8,128)S(1)}) custom-call(f32[32,2048]{1,0:T(8,128)S(1)} %reshape_squeeze.3.refs_0_, f32[8,1152]{1,0:T(8,128)S(1)} %select_maximum_fusion.refs_1_), custom_call_target="tpu_custom_call" | custom-call | tf_op jit(solution)/shard_map/pallas_call | solution.py:323
  66.4 2.0 copy-done
  68.4 0.1 copy.30
  68.5 0.3 fusion.26
  68.8 0.3 fusion.24
  69.2 0.1 reshape.62
  69.3 0.2 copy.27
  69.5 0.1 reshape.61
  69.6 0.2 bitcast_add_fusion
  69.7 0.1 reshape.63
  69.9 3.9 %fusion.12 = f32[32,1024]{1,0:T(8,128)S(1)} fusion(f32[32,512]{1,0:T(8,128)S(1)} %reshape.63, f32[512,2048]{1,0:T(8,128)} %bitcast.45, f32[1024]{0:T(1024)S(1)} %mul.58), kind=kOutput, calls=%fused_computation.10 | convolution fusion | flops 202997760 | bytes 4395008 | tf_op jit(solution)/shard_map/dot_general | solution.py:561
  73.8 2.2 %copy-done.1 = f32[16,32,2048]{2,1,0:T(8,128)S(1)} copy-done((f32[16,32,2048]{2,1,0:T(8,128)S(1)}, f32[16,32,2048]{2,1,0:T(8,128)}, u32[]{:S(2)}) %copy-start.1) | copy-done | bytes 4194328
  76.0 21.2 %shard_map.75.x = f32[16,32,2048]{2,1,0:T(8,128)S(1)} custom-call(s32[8,3]{1,0:T(8,128)S(1)} %copy.23.tiles_ref, f32[16,32,2048]{2,1,0:T(8,128)S(1)} %copy-done.1, f32[16,32,2048]{2,1,0:T(8,128)S(1)} %copy-done.1, f32[16,32,1024]{2,1,0:T(8,128)S(1)} %get-tuple-element.10.cos_ref, f32[16,32,1024]{2,1,0:T(8,128)S(1)} %copy-done.4, ...), custom_call_target="tpu_custom_call" | custom-call | flops 4831838208 | bytes 12058624 | tf_op jit(solution)/shard_map/pallas_call | solution.py:180
  97.2 30.2 %shard_map.76 = f32[32,2048]{1,0:T(8,128)S(1)} custom-call(f32[16,32,2048]{2,1,0:T(8,128)S(1)} %shard_map.75.x), custom_call_target="tpu_custom_call" | custom-call | tf_op jit(solution)/shard_map/pallas_call | solution.py:462
  127.5 32.8 %shard_map.77.grow_ref.gcol_ref = f32[16,32,2048]{2,1,0:T(8,128)S(1)} custom-call(f32[32,2048]{1,0:T(8,128)S(1)} %fusion.28.refs_0_), custom_call_target="tpu_custom_call" | custom-call | tf_op jit(solution)/shard_map/pallas_call | solution.py:323
  160.3 21.2 %shard_map.78.x = f32[16,32,2048]{2,1,0:T(8,128)S(1)} custom-call(s32[8,3]{1,0:T(8,128)S(1)} %copy.23.tiles_ref, f32[16,32,2048]{2,1,0:T(8,128)S(1)} %shard_map.77.grow_ref.gcol_ref, f32[16,32,2048]{2,1,0:T(8,128)S(1)} %shard_map.77.grow_ref.gcol_ref, f32[16,32,1024]{2,1,0:T(8,128)S(1)} %get-tuple-element.10.cos_ref, f32[16,32,1024]{2,1,0:T(8,128)S(1)} %copy-done.4, ...), custom_call_target="tpu_custom_call" | custom-call | flops 4831838208 | bytes 12058624 | tf_op jit(solution)/shard_map/pallas_call | solution.py:180
  181.5 31.1 %shard_map.79 = f32[32,2048]{1,0:T(8,128)S(1)} custom-call(f32[16,32,2048]{2,1,0:T(8,128)S(1)} %shard_map.78.x), custom_call_target="tpu_custom_call" | custom-call | tf_op jit(solution)/shard_map/pallas_call | solution.py:462
  212.6 1.5 fusion.21
  214.2 0.3 reshape_stack.3
  214.5 0.6 copy.29
  215.2 1.2 reshape.66
  (20 shorter events, 0.2 us)
Async XLA Ops:
  8.1 6.3 %copy-start.5 = (f32[16,3,512]{2,0,1:T(8,128)S(1)}, f32[16,3,512]{2,0,1:T(8,128)}, u32[]{:S(2)}) copy-start(f32[16,3,512]{2,0,1:T(8,128)} %param.11) | copy-start | bytes 294916
  17.0 2.2 %copy-start.2 = (f32[16,3,512]{1,2,0:T(8,128)S(1)}, f32[16,3,512]{1,2,0:T(8,128)}, u32[]{:S(2)}) copy-start(f32[16,3,512]{1,2,0:T(8,128)} %copy.20) | copy-start | bytes 294916
  24.1 1.4 copy-start.3
  66.4 2.0 copy-start
  69.9 3.9 %copy-start.4 = (f32[16,32,1024]{2,1,0:T(8,128)S(1)}, f32[16,32,1024]{2,1,0:T(8,128)}, u32[]{:S(2)}) copy-start(f32[16,32,1024]{2,1,0:T(8,128)} %copy-done.3) | copy-start | bytes 6291460
  73.8 2.2 %copy-start.1 = (f32[16,32,2048]{2,1,0:T(8,128)S(1)}, f32[16,32,2048]{2,1,0:T(8,128)}, u32[]{:S(2)}) copy-start(f32[16,32,2048]{2,1,0:T(8,128)} %copy-done) | copy-start | bytes 12582916
